TPU v7x, 256 devices: a whole 4x4x8 slice. The times are simulated.
256 devices in a mesh: wide: 128 (over x, z, y), narrow: 2 (over core).
Axes of the slice: x: 4, y: 4, z: 8, core: 2. Of those that a mesh axis runs over, the one named last changes fastest.
Arguments:
- first_a: float32 [4096, 128], P(('wide', 'narrow')), may hold values from -42 to 42
- first_b: float32 [4096, 128], P(('wide', 'narrow')), may hold values from -42 to 42
- middle_a: float32 [128, 4096, 128], P(None, ('wide', 'narrow')), may hold values from -4.2 to 4.2
- middle_b: float32 [128, 4096, 128], P(None, ('wide', 'narrow')), may hold values from -4.2 to 4.2
- last_a: float32 [128, 4096, 128], P(None, ('wide', 'narrow')), may hold values from -0.5 to 0.5
- last_b: float32 [128, 4096, 128], P(None, ('wide', 'narrow')), may hold values from -0.5 to 0.5
Outputs:
- ortho_first: float32 [4096, 256], P(('wide', 'narrow'))
- ortho_middle: float32 [256, 4096, 256], P(None, ('wide', 'narrow'))
- next_core: float32 [256, 4096, 256], P(None, ('wide', 'narrow'))
All inputs are finite; a program needn't handle non-finite values.
Results may differ from a plain program's by a relative error of at most 0.000086.
Values sent between devices are 32-bit elements; how exact they have to be, the bound alone decides.
A program may use at most 128 MiB of HBM per device.

v0:
```python
import jax
import jax.numpy as jnp
from jax import lax
from jax.sharding import PartitionSpec as P

HIGHEST_PRECISION = lax.Precision.HIGHEST


def gram_matrix(matrix_rows):
    return lax.dot_general(
        matrix_rows,
        matrix_rows,
        (((0,), (0,)), ((), ())),
        precision=HIGHEST_PRECISION,
        preferred_element_type=jnp.float32,
    )


def matmul_exact(matrix_left, matrix_right):
    return jnp.dot(
        matrix_left, matrix_right, precision=HIGHEST_PRECISION, preferred_element_type=jnp.float32
    )


def invert_factor(factor_low):
    identity = jnp.eye(factor_low.shape[0], dtype=jnp.float32)
    inverse_low = jax.scipy.linalg.solve_triangular(factor_low, identity, lower=True)
    return (factor_low.T, inverse_low.T)


def carry_factor(factor_up, block_first, block_second):
    half_rank = block_first.shape[0]
    mode_count = block_first.shape[1]
    shape_block = (half_rank, mode_count, half_rank)
    flat_first = block_first.reshape(half_rank, -1)
    flat_second = block_second.reshape(half_rank, -1)
    top_first = matmul_exact(factor_up[:half_rank, :half_rank], flat_first)
    top_second = matmul_exact(factor_up[:half_rank, half_rank:], flat_second)
    low_second = matmul_exact(factor_up[half_rank:, half_rank:], flat_second)
    upper_rows = jnp.concatenate(
        [top_first.reshape(shape_block), top_second.reshape(shape_block)], axis=2
    )
    lower_rows = jnp.concatenate(
        [jnp.zeros(shape_block, jnp.float32), low_second.reshape(shape_block)], axis=2
    )
    return jnp.concatenate([upper_rows, lower_rows], axis=0)


def body(first_a, first_b, middle_a, middle_b, last_a, last_b):
    devices = lax.axis_size("wide") * lax.axis_size("narrow")
    first_rows = jnp.concatenate([first_a, first_b], axis=1)
    total_one = first_rows.shape[0] * devices
    gram_one = lax.psum(gram_matrix(first_rows), ("wide", "narrow")) / total_one
    factor_one, inverse_one = invert_factor(jnp.linalg.cholesky(gram_one))
    ortho_first = matmul_exact(first_rows, inverse_one)
    carried = carry_factor(factor_one, middle_a, middle_b)
    full_rank = carried.shape[2]
    middle_rows = carried.reshape(-1, full_rank)
    total_two = middle_rows.shape[0] * devices
    gram_two = lax.psum(gram_matrix(middle_rows), ("wide", "narrow")) / total_two
    factor_two, inverse_two = invert_factor(jnp.linalg.cholesky(gram_two))
    ortho_rows = matmul_exact(middle_rows, inverse_two)
    ortho_middle = ortho_rows.reshape(carried.shape)
    next_core = carry_factor(factor_two, last_a, last_b)
    return (ortho_first, ortho_middle, next_core)


def solution(mesh):
    placed = (
        P(("wide", "narrow"), None),
        P(("wide", "narrow"), None),
        P(None, ("wide", "narrow"), None),
        P(None, ("wide", "narrow"), None),
        P(None, ("wide", "narrow"), None),
        P(None, ("wide", "narrow"), None),
    )
    return jax.shard_map(
        body,
        mesh=mesh,
        in_specs=placed,
        out_specs=(
            P(("wide", "narrow"), None),
            P(None, ("wide", "narrow"), None),
            P(None, ("wide", "narrow"), None),
        ),
        check_vma=False,
    )
```

profile of v0, /device:TPU:1, one launch (start us, length us, event | category | flops | bytes accessed | tf_op | source)
XLA Modules:
  0.0 687.5 jit_solution(796027429798825163)
XLA Ops:
  7.2 0.8 constant_dynamic-update-slice_fusion.1
  8.0 0.7 constant_dynamic-update-slice_fusion
  8.7 1.1 fusion.39
  9.9 1.7 copy.60
  11.6 1.3 copy.11
  13.9 1.3 copy.21
  15.2 1.6 copy.59
  17.2 249.6 %all-reduce.6.cloned.1.call-done = f32[256,256]{0,1:T(8,128)} async-done(((f32[256,256]{0,1:T(8,128)}), f32[256,256]{0,1:T(8,128)}) %all-reduce.6.cloned.1.call-update) | async-done | bytes 262160 | tf_op jit(solution)/shard_map/psum | solution.py:53
  266.7 1.0 broadcast_multiply_fusion.1
  267.8 1.0 fusion.8
  268.8 11.7 %cholesky.130 = f32[128,128]{1,0:T(8,128)S(1)} custom-call(f32[128,128]{1,0:T(8,128)S(1)} %cholesky.194), custom_call_target="Cholesky" | custom-call | tf_op jit(solution)/shard_map/jit(cholesky)/cholesky | solution.py:54
  280.6 9.8 %custom-call.13 = f32[1,128,128]{1,2,0:T(8,128)S(1)} custom-call(f32[1,128,128]{2,1,0:T(8,128)S(1)} %get-tuple-element.55), custom_call_target="InvertDiagBlocksLowerTriangular" | custom-call | tf_op jit(solution)/shard_map/jit(cholesky)/cholesky | solution.py:54
  290.9 11.9 %cholesky.147 = f32[128,128]{1,0:T(8,128)S(1)} custom-call(f32[128,128]{1,0:T(8,128)S(1)} %convolution_subtract_fusion.3), custom_call_target="Cholesky" | custom-call | tf_op jit(solution)/shard_map/jit(cholesky)/cholesky | solution.py:54
  302.8 0.7 compare_reduce_fusion.2
  304.7 0.7 fusion.13
  305.5 1.0 fusion.26
  306.4 1.0 fusion.27
  307.4 2.6 fusion.28
  310.0 4.2 convolution_bitcast_fusion
  314.2 3.6 select_maximum_fusion.1
  317.9 5.6 while.4
  318.5 2.2 bitcast_dynamic-update-slice_fusion.4
  321.3 2.1 bitcast_dynamic-update-slice_fusion.4
  323.5 19.7 %custom-call.14 = f32[2,128,128]{1,2,0:T(8,128)S(1)} custom-call(f32[2,128,128]{2,1,0:T(8,128)S(1)} %get-tuple-element.19), custom_call_target="InvertDiagBlocksLowerTriangular" | custom-call | tf_op jit(solution)/shard_map/jit(_solve_triangular)/triangular_solve | solution.py:27
  343.5 1.1 convolution_subtract_fusion.1
  344.9 5.7 copy.36
  350.6 0.9 fusion
  351.5 242.3 %all-reduce.8.cloned.1.call-done = f32[256,256]{0,1:T(8,128)} async-done(((f32[256,256]{0,1:T(8,128)}), f32[256,256]{0,1:T(8,128)}) %all-reduce.8.cloned.1.call-update) | async-done | bytes 262160 | tf_op jit(solution)/shard_map/psum | solution.py:60
  593.8 1.0 broadcast_multiply_fusion
  594.9 1.0 fusion.7
  595.9 11.7 %cholesky.164 = f32[128,128]{1,0:T(8,128)S(1)} custom-call(f32[128,128]{1,0:T(8,128)S(1)} %cholesky.197), custom_call_target="Cholesky" | custom-call | tf_op jit(solution)/shard_map/jit(cholesky)/cholesky | solution.py:61
  607.7 0.6 compare_reduce_fusion.1
  608.3 9.8 %custom-call.15 = f32[1,128,128]{1,2,0:T(8,128)S(1)} custom-call(f32[1,128,128]{2,1,0:T(8,128)S(1)} %get-tuple-element.51), custom_call_target="InvertDiagBlocksLowerTriangular" | custom-call | tf_op jit(solution)/shard_map/jit(cholesky)/cholesky | solution.py:61
  618.6 11.7 %cholesky.181 = f32[128,128]{1,0:T(8,128)S(1)} custom-call(f32[128,128]{1,0:T(8,128)S(1)} %convolution_subtract_fusion.2), custom_call_target="Cholesky" | custom-call | tf_op jit(solution)/shard_map/jit(cholesky)/cholesky | solution.py:61
  630.4 0.6 compare_reduce_fusion
  632.3 0.7 fusion.14
  633.1 1.0 fusion.19
  634.0 1.2 fusion.20
  635.3 5.8 while.5
  635.4 0.6 fusion.61
  636.0 2.3 bitcast_dynamic-update-slice_fusion.5
  638.9 2.2 bitcast_dynamic-update-slice_fusion.5
  641.1 19.7 %custom-call.16 = f32[2,128,128]{1,2,0:T(8,128)S(1)} custom-call(f32[2,128,128]{2,1,0:T(8,128)S(1)} %get-tuple-element.20), custom_call_target="InvertDiagBlocksLowerTriangular" | custom-call | tf_op jit(solution)/shard_map/jit(_solve_triangular)/triangular_solve | solution.py:27
  661.1 1.1 convolution_subtract_fusion
  662.5 2.2 fusion.21
  664.8 2.4 select_maximum_fusion
  667.1 5.4 copy.28
  672.6 7.7 %fusion.4 = f32[256,16,256]{2,1,0:T(8,128)} fusion(f32[256,16,256]{2,1,0:T(8,128)} %copy.36, f32[128,256]{1,0:T(8,128)S(1)} %fusion.23, f32[128,256]{1,0:T(8,128)S(1)} %fusion.15), kind=kOutput, calls=%fused_computation.21 | convolution fusion | flops 3221291008 | bytes 8650752 | tf_op jit(solution)/shard_map/dot_general | solution.py:20
  (46 shorter events, 6.0 us)
Async XLA Ops:
  7.2 5.7 copy-start.1
  7.2 259.5 %all-reduce.6.cloned.1.call-start = ((), (), s32[]{:S(2)}) async-start(), calls=%async_computation | async-start | bytes 524288 | tf_op jit(solution)/shard_map/psum | solution.py:53
  9.8 584.0 %all-reduce.8.cloned.1.call-start = ((), (), s32[]{:S(2)}) async-start(), calls=%async_computation.1 | async-start | bytes 524288 | tf_op jit(solution)/shard_map/psum | solution.py:60
  9.9 3.7 copy-start.2
  307.4 2.6 copy-start
  633.1 2.2 copy-start.3
Sparse Core Ops, SparseCore 0:
  14.0 252.6 all-reduce.5
  345.0 248.7 all-reduce.7
where the time goes:
time: 698 us; the launch traced here: 688 us
  waiting for transfers between devices  492 us (70%)
  other arithmetic  119 us (17%)
  local copies, waits for them, and re-layouts  31.4 us (4%)
  matrix products  27.3 us (4%)
  between operations  17.4 us (2%)
    psum x1, waiting for transfers between devices, body(): gram_one = lax.psum(gram_matrix(first_rows), ('wide', 'narrow')) / total_one  250 us
    psum x1, waiting for transfers between devices, body(): lax.psum(gram_matrix(middle_rows), ('wide', 'narrow')) / total_two  242 us
    another operation x3, other arithmetic, invert_factor(): jax.scipy.linalg.solve_triangular(factor_low, identity, lower=True)  39.4 us
    another operation x7, other arithmetic, body(): factor_two, inverse_two = invert_factor(jnp.linalg.cholesky(gram_two))  34.6 us
    another operation x6, other arithmetic, body(): factor_one, inverse_one = invert_factor(jnp.linalg.cholesky(gram_one))  34.1 us
    dot_general x8, matrix products, matmul_exact(): jnp.dot(matrix_left, matrix_right, precision=HIGHEST_PRECISION, preferred...  17.6 us
  transfers between devices with their start and end apart: 2, of which 2 were waited for; matrix products, arithmetic and copies ran while one was open for 2% of the time, Pallas kernels for 0%

commit v1 on v0

--- a/solution.py
+++ b/solution.py
@@ -1,19 +1,187 @@
+import functools
+
 import jax
 import jax.numpy as jnp
 from jax import lax
+from jax.experimental import pallas as pl
+from jax.experimental.pallas import tpu as pltpu
 from jax.sharding import PartitionSpec as P
 
+MESH = pl.DeviceIdType.MESH
 HIGHEST_PRECISION = lax.Precision.HIGHEST
-
-
-def gram_matrix(matrix_rows):
+PLANE = 32
+DEPTH = 8
+RANK = 128
+FULL = 256
+MODES = 16
+
+
+def dot_f32(left, right, dims):
     return lax.dot_general(
-        matrix_rows,
-        matrix_rows,
-        (((0,), (0,)), ((), ())),
-        precision=HIGHEST_PRECISION,
-        preferred_element_type=jnp.float32,
-    )
+        left, right, (dims, ((), ())), precision=HIGHEST_PRECISION, preferred_element_type=jnp.float32
+    )
+
+
+def gram_kernel(
+    first_a, first_b, middle_a, middle_b, gram_one, gram_two,
+    held_a, held_b, local_one, local_two, total_one, total_two, part_in, piece_out, piece_in,
+    load_sem, send_sem, recv_sem,
+):
+    wide = lax.axis_index("wide")
+    core = lax.axis_index("narrow")
+    spot_x = wide // 32
+    spot_z = (wide // 4) % 8
+    spot_y = wide % 4
+    mine = (spot_x * 4 + spot_y) * 2 + core
+
+    def plane_device(step):
+        peer = (mine + step) % PLANE
+        return peer, ((peer // 8) * 32 + spot_z * 4 + (peer // 2) % 4, peer % 2)
+
+    def line_device(step):
+        return (spot_x * 32 + ((spot_z + step) % DEPTH) * 4 + spot_y, core)
+
+    barrier = pltpu.get_barrier_semaphore()
+
+    def greet_plane(step, carry):
+        pl.semaphore_signal(barrier, inc=1, device_id=plane_device(step)[1], device_id_type=MESH)
+        return carry
+
+    def greet_line(step, carry):
+        pl.semaphore_signal(barrier, inc=1, device_id=line_device(step), device_id_type=MESH)
+        return carry
+
+    lax.fori_loop(1, PLANE, greet_plane, 0)
+    lax.fori_loop(1, DEPTH, greet_line, 0)
+
+    loads = []
+    for mode in range(MODES):
+        for side, (source, target) in enumerate(((middle_a, held_a), (middle_b, held_b))):
+            load = pltpu.make_async_copy(source.at[:, mode, :], target.at[mode], load_sem.at[side, mode])
+            load.start()
+            loads.append(load)
+
+    rows = jnp.concatenate([first_a[...], first_b[...]], axis=1)
+    local_one[...] = dot_f32(rows, rows, ((0,), (0,))).reshape(PLANE, 8, FULL)
+    pl.semaphore_wait(barrier, PLANE - 1 + DEPTH - 1)
+
+    def reduce_all(turn, local, total, scale):
+        def scatter(step, carry):
+            peer, device = plane_device(step)
+            pltpu.make_async_remote_copy(
+                src_ref=local.at[peer],
+                dst_ref=part_in.at[turn, step - 1],
+                send_sem=send_sem.at[turn, 0],
+                recv_sem=recv_sem.at[turn, 0],
+                device_id=device,
+                device_id_type=MESH,
+            ).start()
+            return carry
+
+        lax.fori_loop(1, PLANE, scatter, 0)
+
+        def wait_plane(phase, buffer):
+            copy = pltpu.make_async_remote_copy(
+                src_ref=buffer,
+                dst_ref=buffer,
+                send_sem=send_sem.at[turn, phase],
+                recv_sem=recv_sem.at[turn, phase],
+                device_id=(wide, core),
+                device_id_type=MESH,
+            )
+            copy.wait_recv()
+            copy.wait_send()
+
+        wait_plane(0, part_in.at[turn])
+        piece_out[turn] = local[mine] + jnp.sum(part_in[turn], axis=0)
+
+        def line(step, carry):
+            pltpu.make_async_remote_copy(
+                src_ref=piece_out.at[turn],
+                dst_ref=piece_in.at[turn, step - 1],
+                send_sem=send_sem.at[turn, 1],
+                recv_sem=recv_sem.at[turn, 1],
+                device_id=line_device(step),
+                device_id_type=MESH,
+            ).start()
+            return carry
+
+        lax.fori_loop(1, DEPTH, line, 0)
+        wait_plane(1, piece_in.at[turn])
+        total[mine] = (piece_out[turn] + jnp.sum(piece_in[turn], axis=0)) * scale
+
+        def gather(step, carry):
+            peer, device = plane_device(step)
+            pltpu.make_async_remote_copy(
+                src_ref=total.at[mine],
+                dst_ref=total.at[mine],
+                send_sem=send_sem.at[turn, 2],
+                recv_sem=recv_sem.at[turn, 2],
+                device_id=device,
+                device_id_type=MESH,
+            ).start()
+            return carry
+
+        lax.fori_loop(1, PLANE, gather, 0)
+        wait_plane(2, total.at[pl.ds(0, PLANE - 1)])
+
+    reduce_all(0, local_one, total_one, 1.0 / 4096)
+    gram = total_one[...].reshape(FULL, FULL)
+    gram_one[...] = gram
+    for load in loads:
+        load.wait()
+    gram_aa = gram[:RANK, :RANK]
+    gram_ab = gram[:RANK, RANK:]
+    gram_bb = gram[RANK:, RANK:]
+
+    def carry_mode(mode, sums):
+        sum_aa, sum_ab, sum_bb = sums
+        block_a = held_a[mode]
+        block_b = held_b[mode]
+        over = ((1,), (0,))
+        rows = ((0,), (0,))
+        sum_aa += dot_f32(block_a, dot_f32(gram_aa, block_a, over), rows)
+        sum_ab += dot_f32(block_a, dot_f32(gram_ab, block_b, over), rows)
+        sum_bb += dot_f32(block_b, dot_f32(gram_bb, block_b, over), rows)
+        return sum_aa, sum_ab, sum_bb
+
+    zero = jnp.zeros((RANK, RANK), jnp.float32)
+    sum_aa, sum_ab, sum_bb = lax.fori_loop(0, MODES, carry_mode, (zero, zero, zero))
+    local = jnp.concatenate(
+        [jnp.concatenate([sum_aa, sum_ab], axis=1), jnp.concatenate([sum_ab.T, sum_bb], axis=1)], axis=0
+    )
+    local_two[...] = local.reshape(PLANE, 8, FULL)
+    reduce_all(1, local_two, total_two, 1.0 / 1048576)
+    gram_two[...] = total_two[...].reshape(FULL, FULL)
+
+
+def both_grams(first_a, first_b, middle_a, middle_b):
+    square = jax.ShapeDtypeStruct((FULL, FULL), jnp.float32)
+    vmem = pl.BlockSpec(memory_space=pltpu.VMEM)
+    whole = pl.BlockSpec(memory_space=pl.ANY)
+    return pl.pallas_call(
+        gram_kernel,
+        out_shape=(square, square),
+        in_specs=[vmem, vmem, whole, whole],
+        out_specs=(vmem, vmem),
+        scratch_shapes=[
+            pltpu.VMEM((MODES, RANK, RANK), jnp.float32),
+            pltpu.VMEM((MODES, RANK, RANK), jnp.float32),
+            pltpu.VMEM((PLANE, 8, FULL), jnp.float32),
+            pltpu.VMEM((PLANE, 8, FULL), jnp.float32),
+            pltpu.VMEM((PLANE, 8, FULL), jnp.float32),
+            pltpu.VMEM((PLANE, 8, FULL), jnp.float32),
+            pltpu.VMEM((2, PLANE - 1, 8, FULL), jnp.float32),
+            pltpu.VMEM((2, 8, FULL), jnp.float32),
+            pltpu.VMEM((2, DEPTH - 1, 8, FULL), jnp.float32),
+            pltpu.SemaphoreType.DMA((2, MODES)),
+            pltpu.SemaphoreType.DMA((2, 3)),
+            pltpu.SemaphoreType.DMA((2, 3)),
+        ],
+        compiler_params=pltpu.CompilerParams(
+            collective_id=0, has_side_effects=True, vmem_limit_bytes=32 * 1024 * 1024
+        ),
+    )(first_a, first_b, middle_a, middle_b)
 
 
 def matmul_exact(matrix_left, matrix_right):
@@ -47,17 +215,12 @@
 
 
 def body(first_a, first_b, middle_a, middle_b, last_a, last_b):
-    devices = lax.axis_size("wide") * lax.axis_size("narrow")
+    gram_one, gram_two = both_grams(first_a, first_b, middle_a, middle_b)
     first_rows = jnp.concatenate([first_a, first_b], axis=1)
-    total_one = first_rows.shape[0] * devices
-    gram_one = lax.psum(gram_matrix(first_rows), ("wide", "narrow")) / total_one
     factor_one, inverse_one = invert_factor(jnp.linalg.cholesky(gram_one))
     ortho_first = matmul_exact(first_rows, inverse_one)
     carried = carry_factor(factor_one, middle_a, middle_b)
-    full_rank = carried.shape[2]
-    middle_rows = carried.reshape(-1, full_rank)
-    total_two = middle_rows.shape[0] * devices
-    gram_two = lax.psum(gram_matrix(middle_rows), ("wide", "narrow")) / total_two
+    middle_rows = carried.reshape(-1, FULL)
     factor_two, inverse_two = invert_factor(jnp.linalg.cholesky(gram_two))
     ortho_rows = matmul_exact(middle_rows, inverse_two)
     ortho_middle = ortho_rows.reshape(carried.shape)

time: 698 us -> 211 us (0.30); the launches traced: 688 us -> 208 us
  waiting for transfers between devices: 492 us -> 0 us
  Pallas kernels: 0 us -> 55.3 us
  between operations: 17.4 us -> 3.9 us
  local copies, waits for them, and re-layouts: 31.4 us -> 20.2 us
  matrix products: 27.3 us -> 16.9 us
  other arithmetic: 119 us -> 112 us
    psum x2 -> x0, waiting for transfers between devices: 492 us -> none  [the longest x1 250 us: body(): gram_one = lax.psum(gram_matrix(first_rows), ('wide', 'narrow')) / total_one]
    pallas_call x0 -> x1, Pallas kernels: none -> 55.3 us  [both_grams(): pl.pallas_call(gram_kernel, out_shape=(square, square), in_specs=[vmem, v...]
    another operation x6 -> x7, other arithmetic: 34.1 us -> 34.6 us  [body(): factor_one, inverse_one = invert_factor(jnp.linalg.cholesky(gram_one))]
  transfers between devices with their start and end apart: 2 -> 0, of which waited for: 2 -> 0; matrix products, arithmetic and copies ran while one was open for 2% -> 0% of each run, Pallas kernels for 0% -> 0%
where the time goes in v1:
time: 211 us; the launch traced here: 208 us
  other arithmetic  112 us (53%)
  Pallas kernels  55.3 us (26%)
  local copies, waits for them, and re-layouts  20.2 us (10%)
  matrix products  16.9 us (8%)
  between operations  3.9 us (2%)
    pallas_call x1, Pallas kernels, both_grams(): pl.pallas_call(gram_kernel, out_shape=(square, square), in_specs=[vmem, v...  55.3 us
    another operation x3, other arithmetic, invert_factor(): jax.scipy.linalg.solve_triangular(factor_low, identity, lower=True)  39.6 us
    another operation x7, other arithmetic, body(): factor_two, inverse_two = invert_factor(jnp.linalg.cholesky(gram_two))  34.8 us
    another operation x7, other arithmetic, body(): factor_one, inverse_one = invert_factor(jnp.linalg.cholesky(gram_one))  34.6 us
    dot_general x8, matrix products, matmul_exact(): jnp.dot(matrix_left, matrix_right, precision=HIGHEST_PRECISION, preferred...  14.2 us
    unnamed x25, local copies, waits for them, and re-layouts  11.3 us
    another operation x15, local copies, waits for them, and re-layouts, invert_factor(): jax.scipy.linalg.solve_triangular(factor_low, identity, lower=True)  7.99 us

profile of v1, /device:TPU:1, one launch (start us, length us, event | category | flops | bytes accessed | tf_op | source)
XLA Modules:
  0.0 208.2 jit_solution(2913334342047616778)
XLA Ops:
  0.7 1.2 copy-done
  2.0 1.2 copy-done.2
  3.2 0.7 copy-done.4
  3.9 0.7 copy-done.6
  4.6 55.3 %shard_map.85 = (f32[256,256]{1,0:T(8,128)S(1)}, f32[256,256]{1,0:T(8,128)S(1)}) custom-call(f32[16,128]{1,0:T(8,128)S(1)} %copy-done.4, f32[16,128]{1,0:T(8,128)S(1)} %copy-done.6, f32[128,16,128]{2,1,0:T(8,128)S(1)} %copy-done.2, f32[128,16,128]{2,1,0:T(8,128)S(1)} %copy-done), custom_call_target="tpu_custom_call" | custom-call | tf_op jit(solution)/shard_map/pallas_call | solution.py:162
  60.3 11.7 %cholesky.164 = f32[128,128]{1,0:T(8,128)S(1)} custom-call(f32[128,128]{1,0:T(8,128)S(1)} %cholesky.197), custom_call_target="Cholesky" | custom-call | tf_op jit(solution)/shard_map/jit(cholesky)/cholesky | solution.py:224
  72.0 11.7 %cholesky.130 = f32[128,128]{1,0:T(8,128)S(1)} custom-call(f32[128,128]{1,0:T(8,128)S(1)} %cholesky.194), custom_call_target="Cholesky" | custom-call | tf_op jit(solution)/shard_map/jit(cholesky)/cholesky | solution.py:220
  83.8 0.6 compare_reduce_fusion.3
  84.4 9.8 %custom-call.13 = f32[1,128,128]{1,2,0:T(8,128)S(1)} custom-call(f32[1,128,128]{2,1,0:T(8,128)S(1)} %get-tuple-element.59), custom_call_target="InvertDiagBlocksLowerTriangular" | custom-call | tf_op jit(solution)/shard_map/jit(cholesky)/cholesky | solution.py:220
  94.3 0.6 compare_reduce_fusion.1
  94.9 10.0 %custom-call.15 = f32[1,128,128]{1,2,0:T(8,128)S(1)} custom-call(f32[1,128,128]{2,1,0:T(8,128)S(1)} %get-tuple-element.55), custom_call_target="InvertDiagBlocksLowerTriangular" | custom-call | tf_op jit(solution)/shard_map/jit(cholesky)/cholesky | solution.py:224
  105.1 0.3 convolution_subtract_fusion.2
  105.4 11.7 %cholesky.181 = f32[128,128]{1,0:T(8,128)S(1)} custom-call(f32[128,128]{1,0:T(8,128)S(1)} %convolution_subtract_fusion.2), custom_call_target="Cholesky" | custom-call | tf_op jit(solution)/shard_map/jit(cholesky)/cholesky | solution.py:224
  117.1 0.7 compare_reduce_fusion
  119.4 0.3 convolution_subtract_fusion.3
  119.6 11.7 %cholesky.147 = f32[128,128]{1,0:T(8,128)S(1)} custom-call(f32[128,128]{1,0:T(8,128)S(1)} %convolution_subtract_fusion.3), custom_call_target="Cholesky" | custom-call | tf_op jit(solution)/shard_map/jit(cholesky)/cholesky | solution.py:220
  131.4 0.6 compare_reduce_fusion.2
  133.4 4.0 %while.4 = (s32[]{:T(128)}, f32[256,256]{1,0:T(8,128)S(1)}, s32[2,2]{1,0:T(2,128)S(1)}, f32[2,128,128]{2,1,0:T(8,128)S(1)}, s32[]{:T(128)}) while((s32[]{:T(128)}, f32[256,256]{1,0:T(8,128)S(1)}, s32[2,2]{1,0:T(2,128)S(1)}, f32[2,128,128]{2,1,0:T(8,128)S(1)}, s32[]{:T(128)}) %tuple.50), condition=%wide.while_cond, body=%wide.while_body.sunk | while | flops 2 | bytes 131189 | solution.py:195
  133.4 0.6 fusion.62
  134.0 1.4 bitcast_dynamic-update-slice_fusion.4
  135.4 0.6 fusion.62
  136.0 1.4 bitcast_dynamic-update-slice_fusion.4
  137.4 19.7 %custom-call.14 = f32[2,128,128]{1,2,0:T(8,128)S(1)} custom-call(f32[2,128,128]{2,1,0:T(8,128)S(1)} %get-tuple-element.23), custom_call_target="InvertDiagBlocksLowerTriangular" | custom-call | tf_op jit(solution)/shard_map/jit(_solve_triangular)/triangular_solve | solution.py:195
  157.1 0.3 fusion.27
  157.7 0.3 fusion.37
  158.0 0.9 fusion.11
  159.0 4.0 %while.5 = (s32[]{:T(128)}, f32[256,256]{1,0:T(8,128)S(1)}, s32[2,2]{1,0:T(2,128)S(1)}, f32[2,128,128]{2,1,0:T(8,128)S(1)}, s32[]{:T(128)}) while((s32[]{:T(128)}, f32[256,256]{1,0:T(8,128)S(1)}, s32[2,2]{1,0:T(2,128)S(1)}, f32[2,128,128]{2,1,0:T(8,128)S(1)}, s32[]{:T(128)}) %tuple.56), condition=%wide.while_cond.clone, body=%wide.while_body.clone.sunk | while | flops 2 | bytes 131189 | solution.py:195
  159.1 0.6 fusion.63
  159.7 1.4 bitcast_dynamic-update-slice_fusion.5
  161.1 0.6 fusion.63
  161.7 1.4 bitcast_dynamic-update-slice_fusion.5
  163.0 19.9 %custom-call.16 = f32[2,128,128]{1,2,0:T(8,128)S(1)} custom-call(f32[2,128,128]{2,1,0:T(8,128)S(1)} %get-tuple-element.24), custom_call_target="InvertDiagBlocksLowerTriangular" | custom-call | tf_op jit(solution)/shard_map/jit(_solve_triangular)/triangular_solve | solution.py:195
  182.9 0.3 fusion.25
  183.5 0.3 fusion.33
  183.8 1.3 fusion.5
  185.1 1.3 fusion.7
  186.4 1.3 fusion.2
  187.7 0.4 select_maximum_fusion.1
  188.1 6.5 %fusion = f32[256,16,256]{2,1,0:T(8,128)} fusion(f32[256,16,256]{2,0,1:T(8,128)S(1)} %select_maximum_fusion.1, f32[128,256]{1,0:T(8,128)S(1)} %fusion.33, f32[128,256]{1,0:T(8,128)S(1)} %fusion.25), kind=kOutput, calls=%fused_computation.8 | convolution fusion | flops 3221291008 | bytes 8650752 | tf_op jit(solution)/shard_map/dot_general | solution.py:188
  194.7 0.3 copy.60
  195.0 0.3 copy.11
  195.3 1.0 fusion.31
  196.3 1.6 copy.61
  197.9 0.3 copy.13
  198.3 1.0 fusion.29
  199.3 1.0 fusion.30
  200.2 2.3 %select_maximum_fusion = f32[256,16,256]{0,2,1:T(8,128)} fusion(f32[128,16,128]{0,2,1:T(8,128)S(1)} %fusion.29, f32[128,16,128]{0,2,1:T(8,128)S(1)} %fusion.30, f32[128,16,128]{0,2,1:T(8,128)S(1)} %fusion.31), kind=kLoop, calls=%fused_computation.4 | loop fusion | flops 4194304 | bytes 7340032 | tf_op jit(solution)/shard_map/concatenate | solution.py:214
  202.5 5.4 %copy.18 = f32[256,16,256]{2,1,0:T(8,128)} copy(f32[256,16,256]{0,2,1:T(8,128)} %select_maximum_fusion) | data formatting | bytes 8388608
  (44 shorter events, 1.7 us)
Async XLA Ops:
  0.7 1.2 copy-start
  2.0 1.2 copy-start.2
  3.2 0.7 copy-start.4
  3.9 0.7 copy-start.6
  59.9 98.1 %copy-start.5 = (f32[16,128]{1,0:T(8,128)S(1)}, f32[16,128]{1,0:T(8,128)}, u32[]{:S(2)}) copy-start(f32[16,128]{1,0:T(8,128)} %first_a.1) | copy-start | bytes 24580
  59.9 98.1 %copy-start.7 = (f32[16,128]{1,0:T(8,128)S(1)}, f32[16,128]{1,0:T(8,128)}, u32[]{:S(2)}) copy-start(f32[16,128]{1,0:T(8,128)} %first_b.1) | copy-start | bytes 24580
  72.0 111.8 %copy-start.1 = (f32[128,16,128]{2,1,0:T(8,128)S(1)}, f32[128,16,128]{2,1,0:T(8,128)}, u32[]{:S(2)}) copy-start(f32[128,16,128]{2,1,0:T(8,128)} %middle_b.1) | copy-start | bytes 3145732
  157.4 29.0 %copy-start.3 = (f32[128,16,128]{2,1,0:T(8,128)S(1)}, f32[128,16,128]{2,1,0:T(8,128)}, u32[]{:S(2)}) copy-start(f32[128,16,128]{2,1,0:T(8,128)} %middle_a.1) | copy-start | bytes 3145732
  159.0 36.3 %copy-start.9 = (f32[256,256]{0,1:T(8,128)}, f32[256,256]{0,1:T(8,128)S(1)}, u32[]{:S(2)}) copy-start(f32[256,256]{0,1:T(8,128)S(1)} %get-tuple-element.48) | copy-start | bytes 786436
  188.1 6.5 %copy-start.8 = (f32[128,16,128]{2,1,0:T(8,128)S(1)}, f32[128,16,128]{2,1,0:T(8,128)}, u32[]{:S(2)}) copy-start(f32[128,16,128]{2,1,0:T(8,128)} %param.13) | copy-start | bytes 3145732
  196.3 2.0 copy-start.10

commit v2 on v1

--- a/solution.py
+++ b/solution.py
@@ -14,6 +14,7 @@
 RANK = 128
 FULL = 256
 MODES = 16
+VMEM_BYTES = 60 * 1024 * 1024
 
 
 def dot_f32(left, right, dims):
@@ -24,8 +25,8 @@
 
 def gram_kernel(
     first_a, first_b, middle_a, middle_b, gram_one, gram_two,
-    held_a, held_b, local_one, local_two, total_one, total_two, part_in, piece_out, piece_in,
-    load_sem, send_sem, recv_sem,
+    first_rows, held_a, held_b, local_one, local_two, total_one, total_two, part_in, piece_out, piece_in,
+    first_sem, load_sem, send_sem, recv_sem,
 ):
     wide = lax.axis_index("wide")
     core = lax.axis_index("narrow")
@@ -41,6 +42,12 @@
     def line_device(step):
         return (spot_x * 32 + ((spot_z + step) % DEPTH) * 4 + spot_y, core)
 
+    first_loads = []
+    for side, source in enumerate((first_a, first_b)):
+        load = pltpu.make_async_copy(source, first_rows.at[side], first_sem.at[side])
+        load.start()
+        first_loads.append(load)
+
     barrier = pltpu.get_barrier_semaphore()
 
     def greet_plane(step, carry):
@@ -61,7 +68,9 @@
             load.start()
             loads.append(load)
 
-    rows = jnp.concatenate([first_a[...], first_b[...]], axis=1)
+    for load in first_loads:
+        load.wait()
+    rows = jnp.concatenate([first_rows[0], first_rows[1]], axis=1)
     local_one[...] = dot_f32(rows, rows, ((0,), (0,))).reshape(PLANE, 8, FULL)
     pl.semaphore_wait(barrier, PLANE - 1 + DEPTH - 1)
 
@@ -162,9 +171,10 @@
     return pl.pallas_call(
         gram_kernel,
         out_shape=(square, square),
-        in_specs=[vmem, vmem, whole, whole],
+        in_specs=[whole] * 4,
         out_specs=(vmem, vmem),
         scratch_shapes=[
+            pltpu.VMEM((2, MODES, RANK), jnp.float32),
             pltpu.VMEM((MODES, RANK, RANK), jnp.float32),
             pltpu.VMEM((MODES, RANK, RANK), jnp.float32),
             pltpu.VMEM((PLANE, 8, FULL), jnp.float32),
@@ -174,58 +184,213 @@
             pltpu.VMEM((2, PLANE - 1, 8, FULL), jnp.float32),
             pltpu.VMEM((2, 8, FULL), jnp.float32),
             pltpu.VMEM((2, DEPTH - 1, 8, FULL), jnp.float32),
+            pltpu.SemaphoreType.DMA((2,)),
             pltpu.SemaphoreType.DMA((2, MODES)),
             pltpu.SemaphoreType.DMA((2, 3)),
             pltpu.SemaphoreType.DMA((2, 3)),
         ],
         compiler_params=pltpu.CompilerParams(
-            collective_id=0, has_side_effects=True, vmem_limit_bytes=32 * 1024 * 1024
+            collective_id=0, has_side_effects=True, vmem_limit_bytes=VMEM_BYTES
         ),
     )(first_a, first_b, middle_a, middle_b)
 
 
-def matmul_exact(matrix_left, matrix_right):
-    return jnp.dot(
-        matrix_left, matrix_right, precision=HIGHEST_PRECISION, preferred_element_type=jnp.float32
-    )
-
-
-def invert_factor(factor_low):
-    identity = jnp.eye(factor_low.shape[0], dtype=jnp.float32)
-    inverse_low = jax.scipy.linalg.solve_triangular(factor_low, identity, lower=True)
-    return (factor_low.T, inverse_low.T)
-
-
-def carry_factor(factor_up, block_first, block_second):
-    half_rank = block_first.shape[0]
-    mode_count = block_first.shape[1]
-    shape_block = (half_rank, mode_count, half_rank)
-    flat_first = block_first.reshape(half_rank, -1)
-    flat_second = block_second.reshape(half_rank, -1)
-    top_first = matmul_exact(factor_up[:half_rank, :half_rank], flat_first)
-    top_second = matmul_exact(factor_up[:half_rank, half_rank:], flat_second)
-    low_second = matmul_exact(factor_up[half_rank:, half_rank:], flat_second)
-    upper_rows = jnp.concatenate(
-        [top_first.reshape(shape_block), top_second.reshape(shape_block)], axis=2
-    )
-    lower_rows = jnp.concatenate(
-        [jnp.zeros(shape_block, jnp.float32), low_second.reshape(shape_block)], axis=2
-    )
-    return jnp.concatenate([upper_rows, lower_rows], axis=0)
+def spread_row(tile, row):
+    return jnp.broadcast_to(tile[row : row + 1, :], (8, 128))
+
+
+def spread_lane(tile, lane):
+    return jnp.broadcast_to(tile[:, lane : lane + 1], (8, 128))
+
+
+def eliminate_panel(matrices, uppers, start, stop, lanes, rows):
+    for base in range(start, stop, 8):
+        half, lane = base // 128, base % 128
+        here = base // 8
+        groups = list(range(here, stop // 8))
+        inside = (lanes >= lane) & (lanes < lane + 8)
+        columns = []
+        for matrix in matrices:
+            columns.append({g: [spread_lane(matrix[g][half], lane + t) for t in range(8)] for g in groups})
+            for g in groups:
+                unit = jnp.where(lanes == rows + lane, 1.0, 0.0) if g == here else 0.0
+                matrix[g][half] = jnp.where(inside, unit, matrix[g][half])
+        for t in range(8):
+            live = groups if t < 7 else groups[1:]
+            for matrix, column in zip(matrices, columns):
+                inverse = 1.0 / spread_row(column[here][t], t)
+                factors = {g: column[g][t] * inverse for g in live}
+                if t < 7:
+                    factors[here] = jnp.where(rows > t, factors[here], 0.0)
+                for later in range(t + 1, 8):
+                    entry = spread_row(column[here][later], t)
+                    for g in live:
+                        column[g][later] = column[g][later] - factors[g] * entry
+                for side in (0, 1):
+                    pivot_row = spread_row(matrix[here][side], t)
+                    for g in live:
+                        matrix[g][side] = matrix[g][side] - factors[g] * pivot_row
+        for matrix, upper, column in zip(matrices, uppers, columns):
+            pivots = column[here][0]
+            top = matrix[here][half]
+            for t in range(8):
+                pivots = jnp.where(rows == t, column[here][t], pivots)
+                top = jnp.where(lanes == lane + t, column[here][t], top)
+            root = lax.rsqrt(pivots)
+            top = top * root
+            matrix[here] = [matrix[here][0] * root, matrix[here][1] * root]
+            upper[here] = [top, matrix[here][1]] if half == 0 else [matrix[here][0], top]
+
+
+def factor_squares(squares):
+    panel = 64
+    lanes = lax.broadcasted_iota(jnp.int32, (8, 128), 1)
+    rows = lax.broadcasted_iota(jnp.int32, (8, 128), 0)
+    matrices = [
+        {g: [square[8 * g : 8 * g + 8, :128], square[8 * g : 8 * g + 8, 128:]] for g in range(32)}
+        for square in squares
+    ]
+    uppers = [{} for _ in squares]
+    for start in range(0, FULL, panel):
+        stop = start + panel
+        eliminate_panel(matrices, uppers, start, stop, lanes, rows)
+        if stop == FULL:
+            break
+        row_index = lax.broadcasted_iota(jnp.int32, (panel, FULL), 0) + start
+        lane_index = lax.broadcasted_iota(jnp.int32, (panel, FULL), 1)
+        low = stop // 128 * 128
+        for matrix in matrices:
+            done = jnp.concatenate(
+                [jnp.concatenate(matrix[g], axis=1) for g in range(start // 8, stop // 8)], axis=0
+            )
+            right = jnp.where((lane_index > row_index) & (lane_index < stop), 0.0, done)
+            update = dot_f32(done[:, low:], right, ((0,), (0,)))
+            for g in range(stop // 8, 32):
+                for side in (0, 1):
+                    first, last = start - side * 128, stop - side * 128
+                    kept = matrix[g][side]
+                    if 0 <= first < 128:
+                        kept = jnp.where((lanes >= first) & (lanes < last), 0.0, kept)
+                    matrix[g][side] = kept - update[8 * g - low : 8 * g - low + 8, side * 128 : side * 128 + 128]
+    results = []
+    for matrix, upper in zip(matrices, uppers):
+        factor, inverse = [], []
+        for g in range(32):
+            row = rows + 8 * g
+            factor.append(
+                jnp.concatenate([jnp.where(lanes + 128 * s >= row, upper[g][s], 0.0) for s in (0, 1)], axis=1)
+            )
+            inverse.append(
+                jnp.concatenate([jnp.where(lanes + 128 * s <= row, matrix[g][s], 0.0) for s in (0, 1)], axis=1)
+            )
+        results.append((jnp.concatenate(factor, axis=0), jnp.concatenate(inverse, axis=0)))
+    return results
+
+
+def split(value):
+    high = value.astype(jnp.bfloat16)
+    return high, (value - high.astype(jnp.float32)).astype(jnp.bfloat16)
+
+
+def dot_split(left, right):
+    def dot(one, other):
+        return jnp.dot(one, other, preferred_element_type=jnp.float32)
+
+    return dot(left[0], right[0]) + (dot(left[1], right[0]) + dot(left[0], right[1]))
+
+
+def finish_kernel(
+    gram_one, gram_two, first_a, first_b, middle_a, middle_b, last_a, last_b,
+    ortho_first, ortho_middle, next_core,
+    first, held, carried, following, load_sem, store_sem,
+):
+    loads = []
+    for index, source in enumerate((middle_a, middle_b, last_a, last_b, first_a, first_b)):
+        target = held.at[index] if index < 4 else first.at[index - 4]
+        load = pltpu.make_async_copy(source, target, load_sem.at[index])
+        load.start()
+        loads.append(load)
+    lower = pl.ds(RANK * MODES, RANK * MODES)
+    carried[0, lower] = jnp.zeros((RANK * MODES, RANK), jnp.float32)
+    following[0, lower] = jnp.zeros((RANK * MODES, RANK), jnp.float32)
+
+    (factor_one, inverse_one), (factor_two, inverse_two) = factor_squares([gram_one[...], gram_two[...]])
+    for load in loads:
+        load.wait()
+    first_rows = jnp.concatenate([first[0], first[1]], axis=1)
+    ortho_first[...] = dot_f32(first_rows, inverse_one, ((1,), (1,)))
+
+    def carry(factor, side, target):
+        corner = split(factor[:RANK, :RANK])
+        column = split(factor[:, RANK:])
+        for mode in range(MODES):
+            block_a = split(held[side, pl.ds(mode, RANK, stride=MODES), :])
+            block_b = split(held[side + 1, pl.ds(mode, RANK, stride=MODES), :])
+            target[0, pl.ds(mode, RANK, stride=MODES)] = dot_split(corner, block_a)
+            target[1, pl.ds(mode, FULL, stride=MODES)] = dot_split(column, block_b)
+
+    stores = []
+
+    def send(buffer, target, part):
+        for side in (0, 1):
+            store = pltpu.make_async_copy(
+                buffer.at[side, part], target.at[part, pl.ds(side * RANK, RANK)], store_sem.at[len(stores)]
+            )
+            store.start()
+            stores.append(store)
+
+    carry(factor_two, 2, following)
+    send(following, next_core, pl.ds(0, FULL * MODES))
+    carry(factor_one, 0, carried)
+    inverse = inverse_two.T
+    whole = split(inverse)
+    corner = split(inverse[RANK:, RANK:])
+    step = 512
+    for start in range(0, RANK * MODES, step):
+        part = pl.ds(start, step)
+        result = dot_split(split(jnp.concatenate([carried[0, part], carried[1, part]], axis=1)), whole)
+        carried[0, part] = result[:, :RANK]
+        carried[1, part] = result[:, RANK:]
+        send(carried, ortho_middle, part)
+    for start in range(RANK * MODES, FULL * MODES, step):
+        part = pl.ds(start, step)
+        carried[1, part] = dot_split(split(carried[1, part]), corner)
+        send(carried, ortho_middle, part)
+    for store in stores:
+        store.wait()
+
+
+def finish(gram_one, gram_two, first_a, first_b, *blocks):
+    vmem = pl.BlockSpec(memory_space=pltpu.VMEM)
+    whole = pl.BlockSpec(memory_space=pl.ANY)
+    rows = FULL * MODES
+    flat = [block.reshape(RANK * MODES, RANK) for block in blocks]
+    ortho_first, ortho_middle, next_core = pl.pallas_call(
+        finish_kernel,
+        out_shape=(
+            jax.ShapeDtypeStruct((MODES, FULL), jnp.float32),
+            jax.ShapeDtypeStruct((rows, FULL), jnp.float32),
+            jax.ShapeDtypeStruct((rows, FULL), jnp.float32),
+        ),
+        in_specs=[vmem] * 2 + [whole] * 6,
+        out_specs=(vmem, whole, whole),
+        scratch_shapes=[
+            pltpu.VMEM((2, MODES, RANK), jnp.float32),
+            pltpu.VMEM((4, RANK * MODES, RANK), jnp.float32),
+            pltpu.VMEM((2, rows, RANK), jnp.float32),
+            pltpu.VMEM((2, rows, RANK), jnp.float32),
+            pltpu.SemaphoreType.DMA((6,)),
+            pltpu.SemaphoreType.DMA((18,)),
+        ],
+        compiler_params=pltpu.CompilerParams(vmem_limit_bytes=VMEM_BYTES),
+    )(gram_one, gram_two, first_a, first_b, *flat)
+    shape = (FULL, MODES, FULL)
+    return ortho_first, ortho_middle.reshape(shape), next_core.reshape(shape)
 
 
 def body(first_a, first_b, middle_a, middle_b, last_a, last_b):
     gram_one, gram_two = both_grams(first_a, first_b, middle_a, middle_b)
-    first_rows = jnp.concatenate([first_a, first_b], axis=1)
-    factor_one, inverse_one = invert_factor(jnp.linalg.cholesky(gram_one))
-    ortho_first = matmul_exact(first_rows, inverse_one)
-    carried = carry_factor(factor_one, middle_a, middle_b)
-    middle_rows = carried.reshape(-1, FULL)
-    factor_two, inverse_two = invert_factor(jnp.linalg.cholesky(gram_two))
-    ortho_rows = matmul_exact(middle_rows, inverse_two)
-    ortho_middle = ortho_rows.reshape(carried.shape)
-    next_core = carry_factor(factor_two, last_a, last_b)
-    return (ortho_first, ortho_middle, next_core)
+    return finish(gram_one, gram_two, first_a, first_b, middle_a, middle_b, last_a, last_b)
 
 
 def solution(mesh):

time: 211 us -> 78.3 us (0.37); the launches traced: 208 us -> 78.2 us
  other arithmetic: 112 us -> 0 us
  Pallas kernels: 55.3 us -> 77.6 us
  local copies, waits for them, and re-layouts: 20.2 us -> 0 us
  matrix products: 16.9 us -> 0 us
  between operations: 3.9 us -> 0.64 us
    another operation x17 -> x0, other arithmetic: 109 us -> none  [the longest x3 39.6 us: invert_factor(): jax.scipy.linalg.solve_triangular(factor_low, identity, lower=True)]
    pallas_call x1 -> x2, Pallas kernels: 55.3 us -> 77.6 us  [the longest x1 56.7 us: both_grams(): pl.pallas_call(gram_kernel, out_shape=(square, square), in_specs=[whole]...]
    dot_general x8 -> x0, matrix products: 14.2 us -> none  [matmul_exact(): jnp.dot(matrix_left, matrix_right, precision=HIGHEST_PRECISION, preferred...]
    unnamed x25 -> x0, local copies, waits for them, and re-layouts: 11.3 us -> none
    another operation x19 -> x0, local copies, waits for them, and re-layouts: 8.04 us -> none  [the longest x15 7.99 us: invert_factor(): jax.scipy.linalg.solve_triangular(factor_low, identity, lower=True)]
    another operation x10 -> x0, matrix products: 2.71 us -> none  [the longest x6 1.76 us: invert_factor(): jax.scipy.linalg.solve_triangular(factor_low, identity, lower=True)]
    concatenate x2 -> x0, other arithmetic: 2.68 us -> none  [carry_factor(): return jnp.concatenate([upper_rows, lower_rows], axis=0)]
where the time goes in v2:
time: 78.3 us; the launch traced here: 78.2 us
  Pallas kernels  77.6 us (99%)
    pallas_call x1, Pallas kernels, both_grams(): pl.pallas_call(gram_kernel, out_shape=(square, square), in_specs=[whole]...  56.7 us
    pallas_call x1, Pallas kernels, finish(): pl.pallas_call(finish_kernel, out_shape=(jax.ShapeDtypeStruct((MODES, FUL...  20.9 us

profile of v2, /device:TPU:1, one launch (start us, length us, event | category | flops | bytes accessed | tf_op | source)
XLA Modules:
  0.0 78.2 jit_solution(8418509124804201694)
XLA Ops:
  0.6 56.7 %shard_map.85 = (f32[256,256]{1,0:T(8,128)}, f32[256,256]{1,0:T(8,128)}) custom-call(f32[16,128]{1,0:T(8,128)} %first_a.3, f32[16,128]{1,0:T(8,128)} %first_b.3, f32[128,16,128]{2,1,0:T(8,128)} %middle_a.1, f32[128,16,128]{2,1,0:T(8,128)} %middle_b.1), custom_call_target="tpu_custom_call" | custom-call | tf_op jit(solution)/shard_map/pallas_call | solution.py:171
  57.4 20.9 %shard_map.86 = (f32[16,256]{1,0:T(8,128)}, f32[4096,256]{1,0:T(8,128)}, f32[4096,256]{1,0:T(8,128)}) custom-call(f32[256,256]{1,0:T(8,128)} %get-tuple-element.8.gram_one, f32[256,256]{1,0:T(8,128)} %get-tuple-element.9.gram_two, f32[16,128]{1,0:T(8,128)} %first_a.3, f32[16,128]{1,0:T(8,128)} %first_b.3, f32[2048,128]{1,0:T(8,128)} %bitcast.6, ...), custom_call_target="tpu_custom_call" | custom-call | tf_op jit(solution)/shard_map/pallas_call | solution.py:368

commit v3 on v0

v3 whole, which is shorter than its diff:
```python
import jax
import jax.numpy as jnp
from jax import lax
from jax.experimental import pallas as pl
from jax.experimental.pallas import tpu as pltpu
from jax.sharding import PartitionSpec as P

MESH = pl.DeviceIdType.MESH
HIGHEST_PRECISION = lax.Precision.HIGHEST
PIECES = 32
CHIPS = 16
SIDE = 4
DEPTH = 8
RANK = 128
FULL = 256
MODES = 16
VMEM_BYTES = 60 * 1024 * 1024


def dot_f32(left, right, dims):
    return lax.dot_general(
        left, right, (dims, ((), ())), precision=HIGHEST_PRECISION, preferred_element_type=jnp.float32
    )


def far_first(offsets, sizes):
    def hops(offset):
        return sum(min(step, size - step) for step, size in zip(offset, sizes))

    return sorted((offset for offset in offsets if any(offset)), key=lambda offset: -hops(offset))


PLANE_STEPS = far_first([(x, y) for x in range(SIDE) for y in range(SIDE)], (SIDE, SIDE))
LINE_STEPS = far_first([(z,) for z in range(DEPTH)], (DEPTH,))


def split(value):
    high = value.astype(jnp.bfloat16)
    return high, (value - high.astype(jnp.float32)).astype(jnp.bfloat16)


def dot_half(left, right):
    return jnp.dot(left, right, preferred_element_type=jnp.float32)


def factor_steps(square, widths, refs=None):
    rest = square
    start = 0
    uppers, lowers = [], []
    for panel_rows in widths:
        stop = start + panel_rows
        if refs is not None and start:
            rest = refs[2][pl.ds(start, FULL - start), :]
        halves = [rest[:panel_rows, :128], rest[:panel_rows, 128:]]
        below = rest[panel_rows:]
        done = []
        for base in range(start, stop, 8):
            side, lane = base // 128, base % 128
            height = stop - base
            lanes = lax.broadcasted_iota(jnp.int32, (height, 128), 1)
            rows = lax.broadcasted_iota(jnp.int32, (height, 128), 0)
            columns = [
                jnp.broadcast_to(halves[side][:, lane + t : lane + t + 1], (height, 128)) for t in range(8)
            ]
            inside = (lanes >= lane) & (lanes < lane + 8)
            halves[side] = jnp.where(inside, jnp.where(lanes == rows + lane, 1.0, 0.0), halves[side])
            for t in range(8):
                inverse = 1.0 / columns[t][t : t + 1]
                column = jnp.where(rows > t, columns[t], 0.0)
                factors = column * inverse
                for later in range(t + 1, 8):
                    entry = columns[later][t : t + 1]
                    taken = (column * entry) * inverse if later == t + 1 else factors * entry
                    columns[later] = columns[later] - taken
                halves = [half - factors * half[t : t + 1] for half in halves]
            small, small_lanes = rows[:8], lanes[:8]
            pivots, top = columns[0][:8], halves[side][:8]
            for t in range(8):
                pivots = jnp.where(small == t, columns[t][:8], pivots)
                top = jnp.where(small_lanes == lane + t, columns[t][:8], top)
            root = lax.rsqrt(pivots)
            ready = [half[:8] * root for half in halves]
            done.append(jnp.concatenate(ready, axis=1))
            top = top * root
            upper = [top, ready[1]] if side == 0 else [ready[0], top]
            row = small + base
            uppers.append(
                jnp.concatenate([jnp.where(small_lanes + 128 * s >= row, upper[s], 0.0) for s in (0, 1)], axis=1)
            )
            lowers.append(
                jnp.concatenate([jnp.where(small_lanes + 128 * s <= row, ready[s], 0.0) for s in (0, 1)], axis=1)
            )
            halves = [half[8:] for half in halves]
            if base + 8 == stop and stop < FULL:
                done = jnp.concatenate(done, axis=0)
                row_index = lax.broadcasted_iota(jnp.int32, (panel_rows, FULL), 0) + start
                lane_index = lax.broadcasted_iota(jnp.int32, (panel_rows, FULL), 1)
                right = jnp.where((lane_index > row_index) & (lane_index < stop), 0.0, done)
                low = stop // 128 * 128
                update = dot_f32(done[:, low:], right, ((0,), (0,)))[stop - low :]
                below_lanes = lax.broadcasted_iota(jnp.int32, below.shape, 1)
                rest = jnp.where((below_lanes >= start) & (below_lanes < stop), 0.0, below) - update
                if refs is not None:
                    refs[2][pl.ds(stop, FULL - stop), :] = rest
            if refs is not None:
                refs[0][pl.ds(base, 8), :] = uppers.pop()
                refs[1][pl.ds(base, 8), :] = lowers.pop()
            yield
        start = stop
    yield jnp.concatenate(uppers, axis=0), jnp.concatenate(lowers, axis=0)


def gram_kernel(
    first_a, first_b, middle_a, middle_b, gram_two, factor_one, inverse_one,
    first_rows, held, local_one, local_two, total_one, total_two,
    half_in, half_out, part_in, piece_out, piece_in, pairs, pairs_turned, carried_top, carried_low, rest,
    load_sem, send_sem, recv_sem,
):
    wide = lax.axis_index("wide")
    core = lax.axis_index("narrow")
    spot_x = wide // 32
    spot_z = (wide // 4) % 8
    spot_y = wide % 4
    mine = core * CHIPS + spot_x * SIDE + spot_y
    base = core * CHIPS
    other = (wide, 1 - core)

    def plane_peer(step):
        x, y = (spot_x + step[0]) % SIDE, (spot_y + step[1]) % SIDE
        return base + x * SIDE + y, (x * 32 + spot_z * 4 + y, core)

    def line_device(step):
        return (spot_x * 32 + ((spot_z + step[0]) % DEPTH) * 4 + spot_y, core)

    loads = []
    for index, (source, target) in enumerate(
        ((first_a, first_rows.at[0]), (first_b, first_rows.at[1]), (middle_a, held.at[0]), (middle_b, held.at[1]))
    ):
        load = pltpu.make_async_copy(source, target, load_sem.at[index])
        load.start()
        loads.append(load)

    barrier = pltpu.get_barrier_semaphore()
    for step in LINE_STEPS:
        pl.semaphore_signal(barrier, inc=1, device_id=line_device(step), device_id_type=MESH)
    for step in PLANE_STEPS:
        pl.semaphore_signal(barrier, inc=1, device_id=plane_peer(step)[1], device_id_type=MESH)
    pl.semaphore_signal(barrier, inc=1, device_id=other, device_id_type=MESH)

    loads[0].wait()
    loads[1].wait()
    rows = jnp.concatenate([first_rows[0], first_rows[1]], axis=1)
    local_one[...] = dot_f32(rows, rows, ((0,), (0,))).reshape(PIECES, 8, FULL)
    pl.semaphore_wait(barrier, len(LINE_STEPS) + len(PLANE_STEPS) + 1)

    def reduce_all(turn, local, total, scale, meanwhile):
        def start(phase, source, target, device):
            pltpu.make_async_remote_copy(
                src_ref=source,
                dst_ref=target,
                send_sem=send_sem.at[turn, phase],
                recv_sem=recv_sem.at[turn, phase],
                device_id=device,
                device_id_type=MESH,
            ).start()

        def finish_phase(phase, buffer):
            copy = pltpu.make_async_remote_copy(
                src_ref=buffer,
                dst_ref=buffer,
                send_sem=send_sem.at[turn, phase],
                recv_sem=recv_sem.at[turn, phase],
                device_id=other,
                device_id_type=MESH,
            )
            copy.wait_recv()
            copy.wait_send()

        own_half = pl.ds(base, CHIPS)
        start(0, local.at[pl.ds(CHIPS - base, CHIPS)], half_in.at[turn], other)
        finish_phase(0, half_in.at[turn])
        half_out[turn, own_half] = local[own_half] + half_in[turn]

        for index, step in enumerate(PLANE_STEPS):
            peer, device = plane_peer(step)
            start(1, half_out.at[turn, peer], part_in.at[turn, index], device)
        meanwhile(1)
        finish_phase(1, part_in.at[turn])
        piece_out[turn] = half_out[turn, mine] + jnp.sum(part_in[turn], axis=0)

        for index, step in enumerate(LINE_STEPS):
            start(2, piece_out.at[turn], piece_in.at[turn, index], line_device(step))
        meanwhile(2)
        finish_phase(2, piece_in.at[turn])
        total[mine] = (piece_out[turn] + jnp.sum(piece_in[turn], axis=0)) * scale

        for step in PLANE_STEPS:
            start(3, total.at[mine], total.at[mine], plane_peer(step)[1])
        meanwhile(3)
        finish_phase(3, total.at[pl.ds(0, CHIPS - 1)])
        start(4, total.at[own_half], total.at[own_half], other)
        meanwhile(4)
        finish_phase(4, total.at[own_half])

    def prepare(phase):
        if phase > 1:
            return
        for side in (0, 1):
            loads[2 + side].wait()
            for mode in range(MODES):
                pair = jnp.concatenate(split(held[side, pl.ds(mode, RANK, stride=MODES), :]), axis=1)
                pairs[side, mode] = pair
                pairs_turned[side, :, mode * RANK : (mode + 1) * RANK] = pair.T

    reduce_all(0, local_one, total_one, 1.0 / 4096, prepare)
    gram = total_one[...].reshape(FULL, FULL)
    corner = jnp.concatenate(split(gram[:RANK, :RANK]), axis=1)
    column = jnp.concatenate(split(gram[:, RANK:]), axis=1)
    for mode in range(MODES):
        place = pl.ds(mode * RANK, RANK)
        pair_a, pair_b = pairs[0, mode], pairs[1, mode]
        by_a = dot_half(corner, jnp.concatenate([pair_a, pair_a], axis=0))
        by_b = dot_half(column, jnp.concatenate([pair_b, pair_b], axis=0))
        by_a = by_a[:, :RANK] + by_a[:, RANK:]
        by_b = by_b[:, :RANK] + by_b[:, RANK:]
        high, low = split(jnp.concatenate([by_a, by_b[:RANK]], axis=1))
        carried_top[0, place] = high
        carried_top[1, place] = low
        carried_low[place] = jnp.concatenate(split(by_b[RANK:]), axis=1)
    turned_a, turned_b = pairs_turned[0], pairs_turned[1]
    top = dot_half(turned_a, carried_top[0])
    top = top[:RANK] + (top[RANK:] + dot_half(turned_a[:RANK], carried_top[1]))
    low = dot_half(turned_b, carried_low[...])
    low = low[:RANK, :RANK] + (low[RANK:, :RANK] + (low[:RANK, RANK:] + low[RANK:, RANK:]))
    local_two[pl.ds(0, CHIPS)] = top.reshape(CHIPS, 8, FULL)
    local_two[pl.ds(CHIPS, CHIPS)] = jnp.concatenate([top[:, RANK:].T, low], axis=1).reshape(CHIPS, 8, FULL)
    steps = factor_steps(gram, (88, 88, 80), (factor_one, inverse_one, rest))

    def factorize(phase):
        for _ in range((0, 11, 11, 10, 0)[phase]):
            next(steps)

    reduce_all(1, local_two, total_two, 1.0 / 1048576, factorize)
    gram_two[...] = total_two[...].reshape(FULL, FULL)


def first_stage(first_a, first_b, middle_a, middle_b):
    square = jax.ShapeDtypeStruct((FULL, FULL), jnp.float32)
    vmem = pl.BlockSpec(memory_space=pltpu.VMEM)
    whole = pl.BlockSpec(memory_space=pl.ANY)
    tall = RANK * MODES
    return pl.pallas_call(
        gram_kernel,
        out_shape=(square,) * 3,
        in_specs=[whole] * 4,
        out_specs=(vmem,) * 3,
        scratch_shapes=[
            pltpu.VMEM((2, MODES, RANK), jnp.float32),
            pltpu.VMEM((2, tall, RANK), jnp.float32),
            pltpu.VMEM((PIECES, 8, FULL), jnp.float32),
            pltpu.VMEM((PIECES, 8, FULL), jnp.float32),
            pltpu.VMEM((PIECES, 8, FULL), jnp.float32),
            pltpu.VMEM((PIECES, 8, FULL), jnp.float32),
            pltpu.VMEM((2, CHIPS, 8, FULL), jnp.float32),
            pltpu.VMEM((2, PIECES, 8, FULL), jnp.float32),
            pltpu.VMEM((2, CHIPS - 1, 8, FULL), jnp.float32),
            pltpu.VMEM((2, 8, FULL), jnp.float32),
            pltpu.VMEM((2, DEPTH - 1, 8, FULL), jnp.float32),
            pltpu.VMEM((2, MODES, RANK, FULL), jnp.bfloat16),
            pltpu.VMEM((2, FULL, tall), jnp.bfloat16),
            pltpu.VMEM((2, tall, FULL), jnp.bfloat16),
            pltpu.VMEM((tall, FULL), jnp.bfloat16),
            pltpu.VMEM((FULL, FULL), jnp.float32),
            pltpu.SemaphoreType.DMA((4,)),
            pltpu.SemaphoreType.DMA((2, 5)),
            pltpu.SemaphoreType.DMA((2, 5)),
        ],
        compiler_params=pltpu.CompilerParams(
            collective_id=0, has_side_effects=True, vmem_limit_bytes=VMEM_BYTES
        ),
    )(first_a, first_b, middle_a.reshape(tall, RANK), middle_b.reshape(tall, RANK))


def finish_kernel(
    gram_two, factor_one, inverse_one, first_a, first_b, middle_a, middle_b, last_a, last_b,
    ortho_first, ortho_middle, next_core,
    first, held, carried, following, last_pairs, top_parts, low_pairs, load_sem, store_sem,
):
    loads = []
    for index, source in enumerate((first_a, first_b, middle_a, middle_b, last_a, last_b)):
        target = first.at[index] if index < 2 else held.at[index - 2]
        load = pltpu.make_async_copy(source, target, load_sem.at[index])
        load.start()
        loads.append(load)
    tall = RANK * MODES

    def pair_of(source, mode):
        return jnp.concatenate(split(held[source, pl.ds(mode, RANK, stride=MODES), :]), axis=1)

    def twice(pair):
        return jnp.concatenate([pair, pair], axis=0)

    def factor_pairs(factor):
        corner = jnp.concatenate(split(factor[:RANK, :RANK]), axis=1)
        column = jnp.concatenate(split(factor[:, RANK:]), axis=1)
        return corner, column

    def carry(pairs, block_a, block_b, target, mode):
        by_a = dot_half(pairs[0], twice(block_a))
        by_b = dot_half(pairs[1], twice(block_b))
        target[0, pl.ds(mode, RANK, stride=MODES)] = by_a[:, :RANK] + by_a[:, RANK:]
        target[1, pl.ds(mode, FULL, stride=MODES)] = by_b[:, :RANK] + by_b[:, RANK:]

    stores = []

    def send(buffer, target, part):
        for side in (0, 1):
            store = pltpu.make_async_copy(
                buffer.at[side, part], target.at[part, pl.ds(side * RANK, RANK)], store_sem.at[len(stores)]
            )
            store.start()
            stores.append(store)

    pairs_one = factor_pairs(factor_one[...])

    def begin():
        for load in loads[:4]:
            load.wait()
        first_rows = jnp.concatenate([first[0], first[1]], axis=1)
        ortho_first[...] = dot_f32(first_rows, inverse_one[...], ((1,), (1,)))
        zero = jnp.zeros((tall, RANK), jnp.float32)
        carried[0, pl.ds(tall, tall)] = zero
        following[0, pl.ds(tall, tall)] = zero

    def carry_middle(mode):
        carry(pairs_one, pair_of(0, mode), pair_of(1, mode), carried, mode)

    def prepare_last(mode):
        if mode == 0:
            loads[4].wait()
            loads[5].wait()
        last_pairs[0, mode] = pair_of(2, mode)
        last_pairs[1, mode] = pair_of(3, mode)

    chunk = 512

    def prepare_rows(start):
        part = pl.ds(start, chunk)
        high, low = split(jnp.concatenate([carried[0, part], carried[1, part]], axis=1))
        top_parts[0, part] = high
        top_parts[1, part] = low
        low_pairs[part] = jnp.concatenate(split(carried[1, pl.ds(tall + start, chunk)]), axis=1)

    tasks = [begin]
    tasks += [lambda mode=mode: carry_middle(mode) for mode in range(MODES)]
    tasks += [lambda start=start: prepare_rows(start) for start in range(0, tall, chunk)]
    tasks += [lambda mode=mode: (prepare_last(mode), prepare_last(mode + 1)) for mode in range(0, MODES, 2)]
    steps = factor_steps(gram_two[...], (64, 64, 64, 64))
    for index in range(FULL // 8):
        next(steps)
        if 2 <= index < 2 + len(tasks):
            tasks[index - 2]()
    factor_two, inverse_two = next(steps)

    pairs_two = factor_pairs(factor_two)
    for mode in range(MODES):
        carry(pairs_two, last_pairs[0, mode], last_pairs[1, mode], following, mode)
    send(following, next_core, pl.ds(0, FULL * MODES))
    inverse = inverse_two.T
    high, low = split(inverse)
    corner = twice(jnp.concatenate([high[RANK:, RANK:], low[RANK:, RANK:]], axis=1))
    for start in range(0, tall, chunk):
        part = pl.ds(start, chunk)
        result = dot_half(top_parts[0, part], high) + (
            dot_half(top_parts[1, part], high) + dot_half(top_parts[0, part], low)
        )
        carried[0, part] = result[:, :RANK]
        carried[1, part] = result[:, RANK:]
        send(carried, ortho_middle, part)
    for start in range(0, tall, chunk):
        result = dot_half(low_pairs[pl.ds(start, chunk)], corner)
        part = pl.ds(tall + start, chunk)
        carried[1, part] = result[:, :RANK] + result[:, RANK:]
        send(carried, ortho_middle, part)
    for store in stores:
        store.wait()


def finish(gram_two, factor_one, inverse_one, first_a, first_b, *blocks):
    vmem = pl.BlockSpec(memory_space=pltpu.VMEM)
    whole = pl.BlockSpec(memory_space=pl.ANY)
    rows, tall = FULL * MODES, RANK * MODES
    flat = [block.reshape(tall, RANK) for block in blocks]
    ortho_first, ortho_middle, next_core = pl.pallas_call(
        finish_kernel,
        out_shape=(
            jax.ShapeDtypeStruct((MODES, FULL), jnp.float32),
            jax.ShapeDtypeStruct((rows, FULL), jnp.float32),
            jax.ShapeDtypeStruct((rows, FULL), jnp.float32),
        ),
        in_specs=[vmem] * 3 + [whole] * 6,
        out_specs=(vmem, whole, whole),
        scratch_shapes=[
            pltpu.VMEM((2, MODES, RANK), jnp.float32),
            pltpu.VMEM((4, tall, RANK), jnp.float32),
            pltpu.VMEM((2, rows, RANK), jnp.float32),
            pltpu.VMEM((2, rows, RANK), jnp.float32),
            pltpu.VMEM((2, MODES, RANK, FULL), jnp.bfloat16),
            pltpu.VMEM((2, tall, FULL), jnp.bfloat16),
            pltpu.VMEM((tall, FULL), jnp.bfloat16),
            pltpu.SemaphoreType.DMA((6,)),
            pltpu.SemaphoreType.DMA((18,)),
        ],
        compiler_params=pltpu.CompilerParams(vmem_limit_bytes=VMEM_BYTES),
    )(gram_two, factor_one, inverse_one, first_a, first_b, *flat)
    shape = (FULL, MODES, FULL)
    return ortho_first, ortho_middle.reshape(shape), next_core.reshape(shape)


def body(first_a, first_b, middle_a, middle_b, last_a, last_b):
    gram_two, factor_one, inverse_one = first_stage(first_a, first_b, middle_a, middle_b)
    return finish(gram_two, factor_one, inverse_one, first_a, first_b, middle_a, middle_b, last_a, last_b)


def solution(mesh):
    placed = (
        P(("wide", "narrow"), None),
        P(("wide", "narrow"), None),
        P(None, ("wide", "narrow"), None),
        P(None, ("wide", "narrow"), None),
        P(None, ("wide", "narrow"), None),
        P(None, ("wide", "narrow"), None),
    )
    return jax.shard_map(
        body,
        mesh=mesh,
        in_specs=placed,
        out_specs=(
            P(("wide", "narrow"), None),
            P(None, ("wide", "narrow"), None),
            P(None, ("wide", "narrow"), None),
        ),
        check_vma=False,
    )
```

time: 698 us -> 65.7 us (0.09); the launches traced: 688 us -> 65.5 us
  waiting for transfers between devices: 492 us -> 0 us
  other arithmetic: 119 us -> 0 us
  Pallas kernels: 0 us -> 64.7 us
  local copies, waits for them, and re-layouts: 31.4 us -> 0 us
  matrix products: 27.3 us -> 0 us
  between operations: 17.4 us -> 0.8 us
    psum x2 -> x0, waiting for transfers between devices: 492 us -> none  [the longest x1 250 us: body(): gram_one = lax.psum(gram_matrix(first_rows), ('wide', 'narrow')) / total_one]
    another operation x16 -> x0, other arithmetic: 108 us -> none  [the longest x3 39.4 us: invert_factor(): jax.scipy.linalg.solve_triangular(factor_low, identity, lower=True)]
    pallas_call x0 -> x2, Pallas kernels: none -> 64.7 us  [the longest x1 46.8 us: first_stage(): pl.pallas_call(gram_kernel, out_shape=(square,) * 3, in_specs=[whole] * 4...]
    dot_general x10 -> x0, matrix products: 22.9 us -> none  [the longest x8 17.6 us: matmul_exact(): jnp.dot(matrix_left, matrix_right, precision=HIGHEST_PRECISION, preferred...]
    another operation x19 -> x0, local copies, waits for them, and re-layouts: 11.3 us -> none  [the longest x15 11.3 us: invert_factor(): jax.scipy.linalg.solve_triangular(factor_low, identity, lower=True)]
    unnamed x14 -> x0, local copies, waits for them, and re-layouts: 10.1 us -> none
  transfers between devices with their start and end apart: 2 -> 0, of which waited for: 2 -> 0; matrix products, arithmetic and copies ran while one was open for 2% -> 0% of each run, Pallas kernels for 0% -> 0%
where the time goes in v3:
time: 65.7 us; the launch traced here: 65.5 us
  Pallas kernels  64.7 us (98%)
  between operations  0.8 us (1%)
    pallas_call x1, Pallas kernels, first_stage(): pl.pallas_call(gram_kernel, out_shape=(square,) * 3, in_specs=[whole] * 4...  46.8 us
    pallas_call x1, Pallas kernels, finish(): pl.pallas_call(finish_kernel, out_shape=(jax.ShapeDtypeStruct((MODES, FUL...  17.9 us

profile of v3, /device:TPU:1, one launch (start us, length us, event | category | flops | bytes accessed | tf_op | source)
XLA Modules:
  0.0 65.5 jit_solution(6300375840644974869)
XLA Ops:
  0.6 46.8 %shard_map.85 = (f32[256,256]{1,0:T(8,128)}, f32[256,256]{1,0:T(8,128)}, f32[256,256]{1,0:T(8,128)}) custom-call(f32[16,128]{1,0:T(8,128)} %first_a.3, f32[16,128]{1,0:T(8,128)} %first_b.3, f32[2048,128]{1,0:T(8,128)} %bitcast.6, f32[2048,128]{1,0:T(8,128)} %bitcast.8), custom_call_target="tpu_custom_call" | custom-call | tf_op jit(solution)/shard_map/pallas_call | solution.py:252
  47.4 17.9 %shard_map.86 = (f32[16,256]{1,0:T(8,128)}, f32[4096,256]{1,0:T(8,128)}, f32[4096,256]{1,0:T(8,128)}) custom-call(f32[256,256]{1,0:T(8,128)} %get-tuple-element.9.gram_two, f32[256,256]{1,0:T(8,128)} %get-tuple-element.10.factor_one, f32[256,256]{1,0:T(8,128)} %get-tuple-element.11.inverse_one, f32[16,128]{1,0:T(8,128)} %first_a.3, f32[16,128]{1,0:T(8,128)} %first_b.3, ...), custom_call_target="tpu_custom_call" | custom-call | tf_op jit(solution)/shard_map/pallas_call | solution.py:394

commit v4 on v3

--- a/solution.py
+++ b/solution.py
@@ -43,7 +43,7 @@
     return jnp.dot(left, right, preferred_element_type=jnp.float32)
 
 
-def factor_steps(square, widths, refs=None):
+def factor_steps(square, widths, block, refs=None):
     rest = square
     start = 0
     uppers, lowers = [], []
@@ -54,32 +54,32 @@
         halves = [rest[:panel_rows, :128], rest[:panel_rows, 128:]]
         below = rest[panel_rows:]
         done = []
-        for base in range(start, stop, 8):
+        for base in range(start, stop, block):
             side, lane = base // 128, base % 128
             height = stop - base
             lanes = lax.broadcasted_iota(jnp.int32, (height, 128), 1)
             rows = lax.broadcasted_iota(jnp.int32, (height, 128), 0)
             columns = [
-                jnp.broadcast_to(halves[side][:, lane + t : lane + t + 1], (height, 128)) for t in range(8)
+                jnp.broadcast_to(halves[side][:, lane + t : lane + t + 1], (height, 128)) for t in range(block)
             ]
-            inside = (lanes >= lane) & (lanes < lane + 8)
+            inside = (lanes >= lane) & (lanes < lane + block)
             halves[side] = jnp.where(inside, jnp.where(lanes == rows + lane, 1.0, 0.0), halves[side])
-            for t in range(8):
+            for t in range(block):
                 inverse = 1.0 / columns[t][t : t + 1]
                 column = jnp.where(rows > t, columns[t], 0.0)
                 factors = column * inverse
-                for later in range(t + 1, 8):
+                for later in range(t + 1, block):
                     entry = columns[later][t : t + 1]
                     taken = (column * entry) * inverse if later == t + 1 else factors * entry
                     columns[later] = columns[later] - taken
                 halves = [half - factors * half[t : t + 1] for half in halves]
-            small, small_lanes = rows[:8], lanes[:8]
-            pivots, top = columns[0][:8], halves[side][:8]
-            for t in range(8):
-                pivots = jnp.where(small == t, columns[t][:8], pivots)
-                top = jnp.where(small_lanes == lane + t, columns[t][:8], top)
+            small, small_lanes = rows[:block], lanes[:block]
+            pivots, top = columns[0][:block], halves[side][:block]
+            for t in range(block):
+                pivots = jnp.where(small == t, columns[t][:block], pivots)
+                top = jnp.where(small_lanes == lane + t, columns[t][:block], top)
             root = lax.rsqrt(pivots)
-            ready = [half[:8] * root for half in halves]
+            ready = [half[:block] * root for half in halves]
             done.append(jnp.concatenate(ready, axis=1))
             top = top * root
             upper = [top, ready[1]] if side == 0 else [ready[0], top]
@@ -90,8 +90,8 @@
             lowers.append(
                 jnp.concatenate([jnp.where(small_lanes + 128 * s <= row, ready[s], 0.0) for s in (0, 1)], axis=1)
             )
-            halves = [half[8:] for half in halves]
-            if base + 8 == stop and stop < FULL:
+            halves = [half[block:] for half in halves]
+            if base + block == stop and stop < FULL:
                 done = jnp.concatenate(done, axis=0)
                 row_index = lax.broadcasted_iota(jnp.int32, (panel_rows, FULL), 0) + start
                 lane_index = lax.broadcasted_iota(jnp.int32, (panel_rows, FULL), 1)
@@ -103,8 +103,8 @@
                 if refs is not None:
                     refs[2][pl.ds(stop, FULL - stop), :] = rest
             if refs is not None:
-                refs[0][pl.ds(base, 8), :] = uppers.pop()
-                refs[1][pl.ds(base, 8), :] = lowers.pop()
+                refs[0][pl.ds(base, block), :] = uppers.pop()
+                refs[1][pl.ds(base, block), :] = lowers.pop()
             yield
         start = stop
     yield jnp.concatenate(uppers, axis=0), jnp.concatenate(lowers, axis=0)
@@ -234,7 +234,7 @@
     low = low[:RANK, :RANK] + (low[RANK:, :RANK] + (low[:RANK, RANK:] + low[RANK:, RANK:]))
     local_two[pl.ds(0, CHIPS)] = top.reshape(CHIPS, 8, FULL)
     local_two[pl.ds(CHIPS, CHIPS)] = jnp.concatenate([top[:, RANK:].T, low], axis=1).reshape(CHIPS, 8, FULL)
-    steps = factor_steps(gram, (88, 88, 80), (factor_one, inverse_one, rest))
+    steps = factor_steps(gram, (88, 88, 80), 8, (factor_one, inverse_one, rest))
 
     def factorize(phase):
         for _ in range((0, 11, 11, 10, 0)[phase]):
@@ -284,7 +284,7 @@
 def finish_kernel(
     gram_two, factor_one, inverse_one, first_a, first_b, middle_a, middle_b, last_a, last_b,
     ortho_first, ortho_middle, next_core,
-    first, held, carried, following, last_pairs, top_parts, low_pairs, load_sem, store_sem,
+    zeros, first, held, carried, following, last_pairs, top_parts, low_pairs, load_sem, store_sem,
 ):
     loads = []
     for index, source in enumerate((first_a, first_b, middle_a, middle_b, last_a, last_b)):
@@ -308,10 +308,23 @@
     def carry(pairs, block_a, block_b, target, mode):
         by_a = dot_half(pairs[0], twice(block_a))
         by_b = dot_half(pairs[1], twice(block_b))
-        target[0, pl.ds(mode, RANK, stride=MODES)] = by_a[:, :RANK] + by_a[:, RANK:]
-        target[1, pl.ds(mode, FULL, stride=MODES)] = by_b[:, :RANK] + by_b[:, RANK:]
+        by_a = by_a[:, :RANK] + by_a[:, RANK:]
+        by_b = by_b[:, :RANK] + by_b[:, RANK:]
+        if target is carried:
+            target[0, pl.ds(mode, RANK, stride=MODES)] = by_a
+            target[1, pl.ds(mode, FULL, stride=MODES)] = by_b
+        else:
+            target[0, pl.ds(mode * RANK, RANK)] = by_a
+            target[1, pl.ds(mode * FULL, FULL)] = by_b
+            start_store(target.at[0, pl.ds(mode * RANK, RANK)], next_core.at[pl.ds(0, RANK), mode, pl.ds(0, RANK)])
+            start_store(target.at[1, pl.ds(mode * FULL, FULL)], next_core.at[:, mode, pl.ds(RANK, RANK)])
 
     stores = []
+
+    def start_store(source, target):
+        store = pltpu.make_async_copy(source, target, store_sem.at[len(stores)])
+        store.start()
+        stores.append(store)
 
     def send(buffer, target, part):
         for side in (0, 1):
@@ -330,7 +343,9 @@
         ortho_first[...] = dot_f32(first_rows, inverse_one[...], ((1,), (1,)))
         zero = jnp.zeros((tall, RANK), jnp.float32)
         carried[0, pl.ds(tall, tall)] = zero
-        following[0, pl.ds(tall, tall)] = zero
+        zeros[...] = jnp.zeros_like(zeros)
+        start_store(zeros, next_core.at[pl.ds(RANK, RANK), :, pl.ds(0, RANK)])
+        start_store(carried.at[0, pl.ds(tall, tall)], ortho_middle.at[pl.ds(tall, tall), pl.ds(0, RANK)])
 
     def carry_middle(mode):
         carry(pairs_one, pair_of(0, mode), pair_of(1, mode), carried, mode)
@@ -355,17 +370,16 @@
     tasks += [lambda mode=mode: carry_middle(mode) for mode in range(MODES)]
     tasks += [lambda start=start: prepare_rows(start) for start in range(0, tall, chunk)]
     tasks += [lambda mode=mode: (prepare_last(mode), prepare_last(mode + 1)) for mode in range(0, MODES, 2)]
-    steps = factor_steps(gram_two[...], (64, 64, 64, 64))
-    for index in range(FULL // 8):
+    steps = factor_steps(gram_two[...], (64, 64, 64, 64), 16)
+    for index in range(FULL // 16):
         next(steps)
-        if 2 <= index < 2 + len(tasks):
-            tasks[index - 2]()
+        for task in tasks[2 * index - 2 : 2 * index] if index else []:
+            task()
     factor_two, inverse_two = next(steps)
 
     pairs_two = factor_pairs(factor_two)
     for mode in range(MODES):
         carry(pairs_two, last_pairs[0, mode], last_pairs[1, mode], following, mode)
-    send(following, next_core, pl.ds(0, FULL * MODES))
     inverse = inverse_two.T
     high, low = split(inverse)
     corner = twice(jnp.concatenate([high[RANK:, RANK:], low[RANK:, RANK:]], axis=1))
@@ -381,7 +395,7 @@
         result = dot_half(low_pairs[pl.ds(start, chunk)], corner)
         part = pl.ds(tall + start, chunk)
         carried[1, part] = result[:, :RANK] + result[:, RANK:]
-        send(carried, ortho_middle, part)
+        start_store(carried.at[1, part], ortho_middle.at[part, pl.ds(RANK, RANK)])
     for store in stores:
         store.wait()
 
@@ -396,11 +410,12 @@
         out_shape=(
             jax.ShapeDtypeStruct((MODES, FULL), jnp.float32),
             jax.ShapeDtypeStruct((rows, FULL), jnp.float32),
-            jax.ShapeDtypeStruct((rows, FULL), jnp.float32),
+            jax.ShapeDtypeStruct((FULL, MODES, FULL), jnp.float32),
         ),
         in_specs=[vmem] * 3 + [whole] * 6,
         out_specs=(vmem, whole, whole),
         scratch_shapes=[
+            pltpu.VMEM((RANK, MODES, RANK), jnp.float32),
             pltpu.VMEM((2, MODES, RANK), jnp.float32),
             pltpu.VMEM((4, tall, RANK), jnp.float32),
             pltpu.VMEM((2, rows, RANK), jnp.float32),
@@ -409,7 +424,7 @@
             pltpu.VMEM((2, tall, FULL), jnp.bfloat16),
             pltpu.VMEM((tall, FULL), jnp.bfloat16),
             pltpu.SemaphoreType.DMA((6,)),
-            pltpu.SemaphoreType.DMA((18,)),
+            pltpu.SemaphoreType.DMA((64,)),
         ],
         compiler_params=pltpu.CompilerParams(vmem_limit_bytes=VMEM_BYTES),
     )(gram_two, factor_one, inverse_one, first_a, first_b, *flat)

time: 65.7 us -> 63.9 us (0.973)
  Pallas kernels: 64.7 us -> 62.9 us
    pallas_call x1, Pallas kernels: 17.9 us -> 16.2 us  [finish(): pl.pallas_call(finish_kernel, out_shape=(jax.ShapeDtypeStruct((MODES, FUL...]
where the time goes in v4:
time: 63.9 us; the launch traced here: 63.7 us
  Pallas kernels  62.9 us (98%)
  between operations  0.8 us (1%)
    pallas_call x1, Pallas kernels, first_stage(): pl.pallas_call(gram_kernel, out_shape=(square,) * 3, in_specs=[whole] * 4...  46.8 us
    pallas_call x1, Pallas kernels, finish(): pl.pallas_call(finish_kernel, out_shape=(jax.ShapeDtypeStruct((MODES, FUL...  16.2 us

profile of v4, /device:TPU:1, one launch (start us, length us, event | category | flops | bytes accessed | tf_op | source)
XLA Modules:
  0.0 63.7 jit_solution(16354158906351559317)
XLA Ops:
  0.6 46.8 %shard_map.85 = (f32[256,256]{1,0:T(8,128)}, f32[256,256]{1,0:T(8,128)}, f32[256,256]{1,0:T(8,128)}) custom-call(f32[16,128]{1,0:T(8,128)} %first_a.3, f32[16,128]{1,0:T(8,128)} %first_b.3, f32[2048,128]{1,0:T(8,128)} %bitcast.5, f32[2048,128]{1,0:T(8,128)} %bitcast.7), custom_call_target="tpu_custom_call" | custom-call | tf_op jit(solution)/shard_map/pallas_call | solution.py:252
  47.4 16.2 %shard_map.86 = (f32[16,256]{1,0:T(8,128)}, f32[4096,256]{1,0:T(8,128)}, f32[256,16,256]{2,1,0:T(8,128)}) custom-call(f32[256,256]{1,0:T(8,128)} %get-tuple-element.9.gram_two, f32[256,256]{1,0:T(8,128)} %get-tuple-element.10.factor_one, f32[256,256]{1,0:T(8,128)} %get-tuple-element.11.inverse_one, f32[16,128]{1,0:T(8,128)} %first_a.3, f32[16,128]{1,0:T(8,128)} %first_b.3, ...), custom_call_target="tpu_custom_call" | custom-call | tf_op jit(solution)/shard_map/pallas_call | solution.py:408

commit v5 on v4

--- a/solution.py
+++ b/solution.py
@@ -113,8 +113,8 @@
 def gram_kernel(
     first_a, first_b, middle_a, middle_b, gram_two, factor_one, inverse_one,
     first_rows, held, local_one, local_two, total_one, total_two,
-    half_in, half_out, part_in, piece_out, piece_in, pairs, pairs_turned, carried_top, carried_low, rest,
-    load_sem, send_sem, recv_sem,
+    half_in, half_out, part_in, piece_out, piece_in, pairs, pairs_turned, carried_top, carried_low, rest, factor_held, inverse_held,
+    out_sem, load_sem, send_sem, recv_sem,
 ):
     wide = lax.axis_index("wide")
     core = lax.axis_index("narrow")
@@ -234,14 +234,24 @@
     low = low[:RANK, :RANK] + (low[RANK:, :RANK] + (low[:RANK, RANK:] + low[RANK:, RANK:]))
     local_two[pl.ds(0, CHIPS)] = top.reshape(CHIPS, 8, FULL)
     local_two[pl.ds(CHIPS, CHIPS)] = jnp.concatenate([top[:, RANK:].T, low], axis=1).reshape(CHIPS, 8, FULL)
-    steps = factor_steps(gram, (88, 88, 80), 8, (factor_one, inverse_one, rest))
+    steps = factor_steps(gram, (88, 88, 80), 8, (factor_held, inverse_held, rest))
+
+    outs = [
+        pltpu.make_async_copy(source, target, out_sem.at[index])
+        for index, (source, target) in enumerate(((factor_held, factor_one), (inverse_held, inverse_one)))
+    ]
 
     def factorize(phase):
         for _ in range((0, 11, 11, 10, 0)[phase]):
             next(steps)
+        if phase == 4:
+            for out in outs:
+                out.start()
 
     reduce_all(1, local_two, total_two, 1.0 / 1048576, factorize)
     gram_two[...] = total_two[...].reshape(FULL, FULL)
+    for out in outs:
+        out.wait()
 
 
 def first_stage(first_a, first_b, middle_a, middle_b):
@@ -253,7 +263,7 @@
         gram_kernel,
         out_shape=(square,) * 3,
         in_specs=[whole] * 4,
-        out_specs=(vmem,) * 3,
+        out_specs=(vmem, whole, whole),
         scratch_shapes=[
             pltpu.VMEM((2, MODES, RANK), jnp.float32),
             pltpu.VMEM((2, tall, RANK), jnp.float32),
@@ -271,6 +281,9 @@
             pltpu.VMEM((2, tall, FULL), jnp.bfloat16),
             pltpu.VMEM((tall, FULL), jnp.bfloat16),
             pltpu.VMEM((FULL, FULL), jnp.float32),
+            pltpu.VMEM((FULL, FULL), jnp.float32),
+            pltpu.VMEM((FULL, FULL), jnp.float32),
+            pltpu.SemaphoreType.DMA((2,)),
             pltpu.SemaphoreType.DMA((4,)),
             pltpu.SemaphoreType.DMA((2, 5)),
             pltpu.SemaphoreType.DMA((2, 5)),
@@ -284,11 +297,12 @@
 def finish_kernel(
     gram_two, factor_one, inverse_one, first_a, first_b, middle_a, middle_b, last_a, last_b,
     ortho_first, ortho_middle, next_core,
-    zeros, first, held, carried, following, last_pairs, top_parts, low_pairs, load_sem, store_sem,
+    squares, zeros, first, held, carried, following, last_pairs, top_parts, low_pairs, load_sem, store_sem,
 ):
     loads = []
-    for index, source in enumerate((first_a, first_b, middle_a, middle_b, last_a, last_b)):
-        target = first.at[index] if index < 2 else held.at[index - 2]
+    places = [squares.at[0], squares.at[1], first.at[0], first.at[1]] + [held.at[index] for index in range(4)]
+    sources = (factor_one, inverse_one, first_a, first_b, middle_a, middle_b, last_a, last_b)
+    for index, (source, target) in enumerate(zip(sources, places)):
         load = pltpu.make_async_copy(source, target, load_sem.at[index])
         load.start()
         loads.append(load)
@@ -334,13 +348,14 @@
             store.start()
             stores.append(store)
 
-    pairs_one = factor_pairs(factor_one[...])
+    pairs_one = []
 
     def begin():
-        for load in loads[:4]:
+        for load in loads[:6]:
             load.wait()
+        pairs_one.extend(factor_pairs(squares[0]))
         first_rows = jnp.concatenate([first[0], first[1]], axis=1)
-        ortho_first[...] = dot_f32(first_rows, inverse_one[...], ((1,), (1,)))
+        ortho_first[...] = dot_f32(first_rows, squares[1], ((1,), (1,)))
         zero = jnp.zeros((tall, RANK), jnp.float32)
         carried[0, pl.ds(tall, tall)] = zero
         zeros[...] = jnp.zeros_like(zeros)
@@ -352,8 +367,8 @@
 
     def prepare_last(mode):
         if mode == 0:
-            loads[4].wait()
-            loads[5].wait()
+            loads[6].wait()
+            loads[7].wait()
         last_pairs[0, mode] = pair_of(2, mode)
         last_pairs[1, mode] = pair_of(3, mode)
 
@@ -412,9 +427,10 @@
             jax.ShapeDtypeStruct((rows, FULL), jnp.float32),
             jax.ShapeDtypeStruct((FULL, MODES, FULL), jnp.float32),
         ),
-        in_specs=[vmem] * 3 + [whole] * 6,
+        in_specs=[vmem] + [whole] * 8,
         out_specs=(vmem, whole, whole),
         scratch_shapes=[
+            pltpu.VMEM((2, FULL, FULL), jnp.float32),
             pltpu.VMEM((RANK, MODES, RANK), jnp.float32),
             pltpu.VMEM((2, MODES, RANK), jnp.float32),
             pltpu.VMEM((4, tall, RANK), jnp.float32),
@@ -423,7 +439,7 @@
             pltpu.VMEM((2, MODES, RANK, FULL), jnp.bfloat16),
             pltpu.VMEM((2, tall, FULL), jnp.bfloat16),
             pltpu.VMEM((tall, FULL), jnp.bfloat16),
-            pltpu.SemaphoreType.DMA((6,)),
+            pltpu.SemaphoreType.DMA((8,)),
             pltpu.SemaphoreType.DMA((64,)),
         ],
         compiler_params=pltpu.CompilerParams(vmem_limit_bytes=VMEM_BYTES),

time: 63.9 us -> 63.8 us (level)
  no operation moved by 1% of the time
where the time goes in v5:
time: 63.8 us; the launch traced here: 63.7 us
  Pallas kernels  62.9 us (99%)
  between operations  0.8 us (1%)
    pallas_call x1, Pallas kernels, first_stage(): pl.pallas_call(gram_kernel, out_shape=(square,) * 3, in_specs=[whole] * 4...  46.6 us
    pallas_call x1, Pallas kernels, finish(): pl.pallas_call(finish_kernel, out_shape=(jax.ShapeDtypeStruct((MODES, FUL...  16.3 us

profile of v5, /device:TPU:1, one launch (start us, length us, event | category | flops | bytes accessed | tf_op | source)
XLA Modules:
  0.0 63.7 jit_solution(9187863205309672831)
XLA Ops:
  0.6 46.6 %shard_map.85 = (f32[256,256]{1,0:T(8,128)}, f32[256,256]{1,0:T(8,128)}, f32[256,256]{1,0:T(8,128)}) custom-call(f32[16,128]{1,0:T(8,128)} %first_a.3, f32[16,128]{1,0:T(8,128)} %first_b.3, f32[2048,128]{1,0:T(8,128)} %bitcast.5, f32[2048,128]{1,0:T(8,128)} %bitcast.7), custom_call_target="tpu_custom_call" | custom-call | tf_op jit(solution)/shard_map/pallas_call | solution.py:262
  47.2 16.3 %shard_map.86 = (f32[16,256]{1,0:T(8,128)}, f32[4096,256]{1,0:T(8,128)}, f32[256,16,256]{2,1,0:T(8,128)}) custom-call(f32[256,256]{1,0:T(8,128)} %get-tuple-element.9.gram_two, f32[256,256]{1,0:T(8,128)} %get-tuple-element.10.factor_one, f32[256,256]{1,0:T(8,128)} %get-tuple-element.11.inverse_one, f32[16,128]{1,0:T(8,128)} %first_a.3, f32[16,128]{1,0:T(8,128)} %first_b.3, ...), custom_call_target="tpu_custom_call" | custom-call | tf_op jit(solution)/shard_map/pallas_call | solution.py:423

commit v6 on v5

--- a/solution.py
+++ b/solution.py
@@ -153,6 +153,8 @@
     local_one[...] = dot_f32(rows, rows, ((0,), (0,))).reshape(PIECES, 8, FULL)
     pl.semaphore_wait(barrier, len(LINE_STEPS) + len(PLANE_STEPS) + 1)
 
+    sent = []
+
     def reduce_all(turn, local, total, scale, meanwhile):
         def start(phase, source, target, device):
             pltpu.make_async_remote_copy(
@@ -174,7 +176,7 @@
                 device_id_type=MESH,
             )
             copy.wait_recv()
-            copy.wait_send()
+            sent.append(copy)
 
         own_half = pl.ds(base, CHIPS)
         start(0, local.at[pl.ds(CHIPS - base, CHIPS)], half_in.at[turn], other)
@@ -252,6 +254,8 @@
     gram_two[...] = total_two[...].reshape(FULL, FULL)
     for out in outs:
         out.wait()
+    for copy in sent:
+        copy.wait_send()
 
 
 def first_stage(first_a, first_b, middle_a, middle_b):

time: 63.8 us -> 63.3 us (level)
  no operation moved by 1% of the time
where the time goes in v6:
time: 63.3 us; the launch traced here: 63.1 us
  Pallas kernels  62.4 us (99%)
  between operations  0.8 us (1%)
    pallas_call x1, Pallas kernels, first_stage(): pl.pallas_call(gram_kernel, out_shape=(square,) * 3, in_specs=[whole] * 4...  46.1 us
    pallas_call x1, Pallas kernels, finish(): pl.pallas_call(finish_kernel, out_shape=(jax.ShapeDtypeStruct((MODES, FUL...  16.3 us

profile of v6, /device:TPU:1, one launch (start us, length us, event | category | flops | bytes accessed | tf_op | source)
XLA Modules:
  0.0 63.1 jit_solution(8202437458879126021)
XLA Ops:
  0.6 46.1 %shard_map.85 = (f32[256,256]{1,0:T(8,128)}, f32[256,256]{1,0:T(8,128)}, f32[256,256]{1,0:T(8,128)}) custom-call(f32[16,128]{1,0:T(8,128)} %first_a.3, f32[16,128]{1,0:T(8,128)} %first_b.3, f32[2048,128]{1,0:T(8,128)} %bitcast.5, f32[2048,128]{1,0:T(8,128)} %bitcast.7), custom_call_target="tpu_custom_call" | custom-call | tf_op jit(solution)/shard_map/pallas_call | solution.py:266
  46.7 16.3 %shard_map.86 = (f32[16,256]{1,0:T(8,128)}, f32[4096,256]{1,0:T(8,128)}, f32[256,16,256]{2,1,0:T(8,128)}) custom-call(f32[256,256]{1,0:T(8,128)} %get-tuple-element.9.gram_two, f32[256,256]{1,0:T(8,128)} %get-tuple-element.10.factor_one, f32[256,256]{1,0:T(8,128)} %get-tuple-element.11.inverse_one, f32[16,128]{1,0:T(8,128)} %first_a.3, f32[16,128]{1,0:T(8,128)} %first_b.3, ...), custom_call_target="tpu_custom_call" | custom-call | tf_op jit(solution)/shard_map/pallas_call | solution.py:427
